TPU v7x, 32 devices: a whole 2x2x4 slice. The times are simulated.
32 devices in a mesh: groups: 2 (over y), expert: 16 (over z, x, core), sub: 1.
Axes of the slice: x: 2, y: 2, z: 4, core: 2. Of those that a mesh axis runs over, the one named last changes fastest.
Arguments:
- tokens: bfloat16 [2048, 2048], P(('groups', 'expert', 'sub')), parts along dimension 0, may hold values from -6 to 6
- router_probs: float32 [2048, 8], P(('groups', 'expert', 'sub')), parts along dimension 0, may hold values from 0.05 to 1
- expert_ids: int32 [2048, 8], P(('groups', 'expert', 'sub')), parts along dimension 0, may hold values from 0 to 15, all different within a row; in each aligned block of 64 rows (0 to 63, 64 to 127, ...) at most 32 rows name the same one
- slot_expert: int32 [16], replicated, may hold values from 0 to 15, each once
- w_gate: bfloat16 [16, 2048, 768], P('expert', None, 'sub'), may hold values from -0.125 to 0.125
- w_up: bfloat16 [16, 2048, 768], P('expert', None, 'sub'), may hold values from -0.125 to 0.125
- w_down: bfloat16 [16, 768, 2048], P('expert', 'sub'), may hold values from -0.21875 to 0.21875
Outputs:
- mixed: bfloat16 [2048, 2048], P(('groups', 'expert', 'sub')), parts along dimension 0
There are 2 independent parts, one for each index of `groups`. A program takes and returns all parts, laid end to end along the dimension named above; an argument that names none is the same for every part. Nothing has to cross between parts.
Inputs may be any that keep to these rules, and one draw needn't show every extreme that they name: `expert_ids`: each row names 8 different experts. Among the rows of one device (aligned blocks of 64 rows) no expert is named more than 32 times, a bound that some block reaches. `slot_expert`: each expert stands in exactly one slot.
All inputs are finite; a program needn't handle non-finite values.
Results may differ from a plain program's by a relative error of at most 0.013.
Values may be sent and summed in bfloat16 or wider, within the bound.
A program may use at most 64 MiB of HBM per device.

v0:
```python
import jax
import jax.numpy as jnp
from jax import lax
from jax.sharding import PartitionSpec as P


def local(tokens, router_probs, expert_ids, slot_expert, w_gate, w_up, w_down):
    tok_rows, width = tokens.shape
    top = expert_ids.shape[1]
    experts = slot_expert.shape[0]
    capacity = min(tok_rows, max(2, (tok_rows * top + experts - 1) // experts))
    gates = router_probs / jnp.sum(router_probs, axis=1, keepdims=True)
    flat_ids = expert_ids.reshape(-1)
    numbers = jnp.arange(experts, dtype=jnp.int32)
    slot_of = jnp.sum(
        jnp.where(slot_expert[None, :] == flat_ids[:, None], numbers[None, :], 0), axis=1
    )
    hits = (flat_ids[:, None] == numbers[None, :]).astype(jnp.int32)
    before = jnp.cumsum(hits, axis=0) - hits
    rank = jnp.sum(before * hits, axis=1)
    target = slot_of * capacity + rank
    select = (target[:, None] == jnp.arange(experts * capacity, dtype=jnp.int32)[None, :]).astype(
        jnp.float32
    )
    select = select.reshape(tok_rows, top, experts * capacity)
    spread = jnp.sum(select, axis=1).astype(jnp.bfloat16)
    weights_mix = jnp.einsum("tk,tkr->tr", gates, select)
    outgoing = jnp.einsum("tr,td->rd", spread, tokens, preferred_element_type=jnp.float32).astype(
        jnp.bfloat16
    )
    outgoing = outgoing.reshape(experts, capacity, width)
    arrived = lax.all_to_all(outgoing, "expert", split_axis=0, concat_axis=0, tiled=True)
    both = lax.all_gather(arrived, "sub", axis=0, tiled=True).reshape(-1, width)
    gate_in = jnp.dot(both, w_gate[0], preferred_element_type=jnp.float32)
    up_in = jnp.dot(both, w_up[0], preferred_element_type=jnp.float32)
    hidden = (jax.nn.silu(gate_in) * up_in).astype(jnp.bfloat16)
    summed = lax.psum_scatter(
        jnp.dot(hidden, w_down[0], preferred_element_type=jnp.float32).astype(jnp.bfloat16),
        "sub",
        scatter_dimension=0,
        tiled=True,
    )
    returned = lax.all_to_all(
        summed.reshape(experts, capacity, width), "expert", split_axis=0, concat_axis=0, tiled=True
    )
    outputs = returned.reshape(experts * capacity, width)
    weight_high = weights_mix.astype(jnp.bfloat16)
    weight_low = (weights_mix - weight_high.astype(jnp.float32)).astype(jnp.bfloat16)
    mixed = jnp.dot(weight_high, outputs, preferred_element_type=jnp.float32)
    mixed = mixed + jnp.dot(weight_low, outputs, preferred_element_type=jnp.float32)
    return mixed.astype(jnp.bfloat16)


def solution(mesh):
    placed = (
        P(("groups", "expert", "sub"), None),
        P(("groups", "expert", "sub"), None),
        P(("groups", "expert", "sub"), None),
        P(),
        P("expert", None, "sub"),
        P("expert", None, "sub"),
        P("expert", "sub", None),
    )
    return jax.shard_map(
        local,
        mesh=mesh,
        in_specs=placed,
        out_specs=P(("groups", "expert", "sub"), None),
        check_vma=False,
    )
```

profile of v0, /device:TPU:11, one launch (start us, length us, event | category | flops | bytes accessed | tf_op | source)
XLA Modules:
  0.0 129.6 jit_solution(15920064002073766494)
XLA Ops:
  0.0 0.0 copy-start
  0.0 0.9 copy.11
  0.9 0.1 eq.52
  1.0 0.1 eq.48
  1.1 1.2 reduce-window.6
  2.3 0.2 slice_reduce_fusion
  2.5 0.8 select_reduce_fusion
  3.3 0.1 add.19
  3.4 0.4 convert_reduce_fusion
  3.8 1.7 %convolution_convert_fusion = bf16[512,2048]{1,0:T(8,128)(2,1)S(1)} fusion(bf16[64,2048]{1,0:T(8,128)(2,1)} %param.7, bf16[64,512]{1,0:T(8,128)(2,1)S(1)} %convert_reduce_fusion), kind=kOutput, calls=%fused_computation.7 | convolution fusion | flops 135266304 | bytes 2424832 | tf_op jit(solution)/shard_map/tr,td->rd/dot_general | solution.py:28
  5.5 0.0 copy-start.3
  5.5 53.9 %all_to_all.10 = bf16[16,32,2048]{2,1,0:T(8,128)(2,1)S(1)} all-to-all(bf16[16,32,2048]{2,1,0:T(8,128)(2,1)S(1)} %bitcast.56), channel_id=1, replica_groups=mesh['groups'=2,'expert'=16,'sub'=1] {'expert'}, dimensions={0} | all-to-all | bytes 4194304 | tf_op jit(solution)/shard_map/all_to_all | solution.py:32
  59.4 0.0 copy-start.1
  59.4 1.3 copy-done.1
  60.7 0.0 copy-done.3
  60.7 3.0 %fusion.4 = f32[512,768]{1,0:T(8,128)} fusion(bf16[512,2048]{1,0:T(8,128)(2,1)S(1)} %bitcast.58, bf16[1,2048,768]{2,1,0:T(8,128)(2,1)S(1)} %copy-done.3), kind=kOutput, calls=%fused_computation.4 | convolution fusion | flops 1610612736 | bytes 6815744 | tf_op jit(solution)/shard_map/dot_general | solution.py:34
  63.7 0.0 copy-done
  63.7 8.3 %fusion.6 = bf16[512,2048]{1,0:T(8,128)(2,1)} fusion(bf16[1,768,2048]{2,1,0:T(8,128)(2,1)S(1)} %copy-done, f32[512,768]{1,0:T(8,128)} %fusion.4, bf16[512,2048]{1,0:T(8,128)(2,1)} %bitcast.59, bf16[1,2048,768]{2,1,0:T(8,128)(2,1)} %param.12), kind=kOutput, calls=%fused_computation.6 | convolution fusion | flops 3224633344 | bytes 12058624 | tf_op jit(solution)/shard_map/dot_general | solution.py:38
  72.0 0.0 copy-start.2
  72.0 5.3 %all-to-all-start.1 = ((bf16[16,32,2048]{2,1,0:T(8,128)(2,1)}), bf16[16,32,2048]{2,1,0:T(8,128)(2,1)}, u32[]{:S(2)}, u32[]{:S(2)}) async-start(bf16[16,32,2048]{2,1,0:T(8,128)(2,1)} %bitcast.57), calls=%async_computation.1 | async-start | bytes 4194304 | tf_op jit(solution)/shard_map/all_to_all | solution.py:43
  77.2 0.0 copy-done.2
  77.2 0.1 copy.14
  77.4 0.3 fusion.12
  77.7 47.0 %all-to-all-done.1 = bf16[16,32,2048]{2,1,0:T(8,128)(2,1)} async-done(((bf16[16,32,2048]{2,1,0:T(8,128)(2,1)}), bf16[16,32,2048]{2,1,0:T(8,128)(2,1)}, u32[]{:S(2)}, u32[]{:S(2)}) %all-to-all-start.1) | async-done | bytes 2097184 | tf_op jit(solution)/shard_map/all_to_all | solution.py:43
  124.7 2.1 %fusion.17 = f32[64,2048]{1,0:T(8,128)S(1)} fusion(bf16[512,2048]{1,0:T(8,128)(2,1)} %bitcast.9, f32[64,1,512]{2,1,0:T(1,128)S(1)} %fusion.12), kind=kOutput, calls=%fused_computation.18 | convolution fusion | flops 134217728 | bytes 2752512 | tf_op jit(solution)/shard_map/dot_general | solution.py:49
  126.8 2.8 %fusion.9 = bf16[64,2048]{1,0:T(8,128)(2,1)} fusion(f32[64,2048]{1,0:T(8,128)S(1)} %fusion.17, bf16[512,2048]{1,0:T(8,128)(2,1)} %bitcast.9, f32[64,1,512]{2,1,0:T(1,128)S(1)} %fusion.12), kind=kOutput, calls=%fused_computation.9 | convolution fusion | flops 134610944 | bytes 3014656 | tf_op jit(solution)/shard_map/dot_general | solution.py:50
  (6 shorter events, 0.1 us)
Async XLA Ops:
  0.0 63.7 %copy-start = (bf16[1,768,2048]{2,1,0:T(8,128)(2,1)S(1)}, bf16[1,768,2048]{2,1,0:T(8,128)(2,1)}, u32[]{:S(2)}) copy-start(bf16[1,768,2048]{2,1,0:T(8,128)(2,1)} %param.13) | copy-start | bytes 9437188
  5.5 55.2 %copy-start.3 = (bf16[1,2048,768]{2,1,0:T(8,128)(2,1)S(1)}, bf16[1,2048,768]{2,1,0:T(8,128)(2,1)}, u32[]{:S(2)}) copy-start(bf16[1,2048,768]{2,1,0:T(8,128)(2,1)} %param.11) | copy-start | bytes 9437188
  59.4 1.3 copy-start.1
  72.0 5.3 %copy-start.2 = (f32[64,8]{0,1:T(8,128)S(1)}, f32[64,8]{0,1:T(8,128)}, u32[]{:S(2)}) copy-start(f32[64,8]{0,1:T(8,128)} %param.8) | copy-start | bytes 6148
  72.0 52.8 %all-to-all-start.1 = ((bf16[16,32,2048]{2,1,0:T(8,128)(2,1)}), bf16[16,32,2048]{2,1,0:T(8,128)(2,1)}, u32[]{:S(2)}, u32[]{:S(2)}) async-start(bf16[16,32,2048]{2,1,0:T(8,128)(2,1)} %bitcast.57), calls=%async_computation.1 | async-start | bytes 4194304 | tf_op jit(solution)/shard_map/all_to_all | solution.py:43
where the time goes:
time: 130 us
  blocking collectives  53.9 us (41%)
  waiting for transfers between devices  47 us (36%)
  matrix products  18.1 us (14%)
  starting transfers between devices  5.25 us (4%)
  local copies, waits for them, and re-layouts  2.82 us (2%)
  other arithmetic  2.36 us (2%)
    all_to_all x1, blocking collectives, local(): lax.all_to_all(outgoing, 'expert', split_axis=0, concat_axis=0, tiled=True)  53.9 us
    all_to_all x1, waiting for transfers between devices, local(): lax.all_to_all(summed.reshape(experts, capacity, width), 'expert', split_...  47 us
    dot_general x1, matrix products, local(): jnp.dot(hidden, w_down[0], preferred_element_type=jnp.float32)  8.28 us
    all_to_all x1, starting transfers between devices, local(): lax.all_to_all(summed.reshape(experts, capacity, width), 'expert', split_...  5.25 us
    dot_general x1, matrix products, local(): gate_in = jnp.dot(both, w_gate[0], preferred_element_type=jnp.float32)  2.97 us
    dot_general x1, matrix products, local(): jnp.dot(weight_low, outputs, preferred_element_type=jnp.float32)  2.78 us
  transfers between devices with their start and end apart: 1, of which 1 were waited for; matrix products, arithmetic and copies ran while one was open for 0% of the time, Pallas kernels for 0%

commit v1 on v0

--- a/solution.py
+++ b/solution.py
@@ -1,7 +1,13 @@
 import jax
 import jax.numpy as jnp
 from jax import lax
+from jax.experimental import pallas as pl
+from jax.experimental.pallas import tpu as pltpu
 from jax.sharding import PartitionSpec as P
+
+RING = 8
+FF_TILE = 256
+D_TILE = 512
 
 
 def local(tokens, router_probs, expert_ids, slot_expert, w_gate, w_up, w_down):
@@ -51,6 +57,266 @@
     return mixed.astype(jnp.bfloat16)
 
 
+def ring_place(e):
+    z, x, core = lax.div(e, 4), lax.rem(lax.div(e, 2), 2), lax.rem(e, 2)
+    return x * (RING - 1 - z) + (1 - x) * z, core
+
+
+def ring_index(place, core):
+    x = lax.div(place, RING // 2)
+    z = x * (RING - 1 - place) + (1 - x) * place
+    return z * 4 + x * 2 + core
+
+
+def long_slot(s):
+    return 2 * s - 1 if s else 0
+
+
+def short_slot(s):
+    return 2 * s
+
+
+def other_slot(slot):
+    if slot in (0, RING - 1):
+        return slot
+    return slot + 1 if slot % 2 else slot - 1
+
+
+def kernel(
+    tokens, probs, ids, slots, w_gate, w_up, w_down, out,
+    x, mix, vg, vu, vd, hidden, own, away, near, long_out, long_in, short_out, short_in,
+    w_sem, ag_send, ag_recv, sib_send, sib_recv, near_send, near_recv,
+    long_send, long_recv, short_send, short_recv,
+):
+    rows, width = tokens.shape
+    half = rows // 2
+    ff = hidden.shape[1]
+    me = lax.axis_index("expert")
+    place, core = ring_place(me)
+    step = 1 - 2 * core
+    ahead = ring_index(lax.rem(place + step + RING, RING), core)
+    behind = ring_index(lax.rem(place - step + RING, RING), core)
+    sibling = me + step
+
+    def device(e):
+        return (lax.axis_index("groups"), e, lax.axis_index("sub"))
+
+    def remote(src, dst, send, recv, e):
+        return pltpu.make_async_remote_copy(
+            src_ref=src, dst_ref=dst, send_sem=send, recv_sem=recv,
+            device_id=device(e), device_id_type=pl.DeviceIdType.MESH,
+        )
+
+    barrier = pltpu.get_barrier_semaphore()
+    for e in (ahead, behind, sibling):
+        pl.semaphore_signal(barrier, inc=1, device_id=device(e), device_id_type=pl.DeviceIdType.MESH)
+
+    loads = [
+        pltpu.make_async_copy(w_gate.at[0], vg, w_sem.at[0]),
+        pltpu.make_async_copy(w_up.at[0], vu, w_sem.at[1]),
+        pltpu.make_async_copy(w_down.at[0], vd, w_sem.at[2]),
+    ]
+    for load in loads:
+        load.start()
+
+    x[0:rows, :] = tokens[...]
+    p = probs[...]
+    gates = p / jnp.sum(p, axis=0, keepdims=True)
+    experts = mix.shape[2]
+    number = lax.broadcasted_iota(jnp.int32, (experts, rows), 0)
+    held = jnp.zeros((experts, rows), jnp.int32)
+    for j in range(experts):
+        held = jnp.where(number == j, slots[j], held)
+    weight = jnp.zeros((experts, rows), jnp.float32)
+    for k in range(p.shape[0]):
+        weight = weight + jnp.where(ids[k:k + 1, :] == held, gates[k:k + 1, :], 0.0)
+    mix[0, 0, :, 0:rows] = weight
+    mix[0, 0, :, rows:] = jnp.zeros((experts, mix.shape[3] - rows), jnp.float32)
+
+    pl.semaphore_wait(barrier, 3)
+
+    def view(slot, side, part):
+        if part == 2:
+            return mix.at[slot, side]
+        return x.at[pl.ds(slot * 2 * rows + side * rows + part * half, half), :]
+
+    PARTS = (2, 0, 1)
+    sends = []
+
+    def ring_copy(src, dst, part, e):
+        return remote(view(src, 0, part), view(dst, 0, part), ag_send.at[dst, part], ag_recv.at[dst, part], e)
+
+    def sib_copy(slot, part):
+        dst = other_slot(slot)
+        return remote(view(slot, 0, part), view(dst, 1, part), sib_send.at[dst, part], sib_recv.at[dst, part], sibling)
+
+    def start(copy):
+        copy.start()
+        sends.append(copy)
+
+    for part in PARTS:
+        start(ring_copy(0, long_slot(1), part, ahead))
+        start(ring_copy(0, short_slot(1), part, behind))
+    for part in PARTS:
+        start(sib_copy(0, part))
+
+    def await_sib(slot, part):
+        remote(view(other_slot(slot), 0, part), view(slot, 1, part), sib_send.at[slot, part], sib_recv.at[slot, part], sibling).wait_recv()
+
+    def arrive(s, parts):
+        for part in parts:
+            ring_copy(long_slot(s - 1), long_slot(s), part, ahead).wait_recv()
+            if s < RING // 2:
+                start(ring_copy(long_slot(s), long_slot(s + 1), part, ahead))
+            start(sib_copy(long_slot(s), part))
+            if s < RING // 2:
+                ring_copy(short_slot(s - 1), short_slot(s), part, behind).wait_recv()
+                if s < RING // 2 - 1:
+                    start(ring_copy(short_slot(s), short_slot(s + 1), part, behind))
+                start(sib_copy(short_slot(s), part))
+
+    def first_half(group):
+        for slot in group:
+            for part in PARTS:
+                await_sib(slot, part)
+        base, count = group[0] * 2 * rows, len(group) * 2 * rows
+
+        @pl.loop(0, ff // FF_TILE)
+        def _(j):
+            cols = pl.ds(pl.multiple_of(j * FF_TILE, FF_TILE), FF_TILE)
+            a = x[base:base + count, :]
+            g = jnp.dot(a, vg[:, cols], preferred_element_type=jnp.float32)
+            u = jnp.dot(a, vu[:, cols], preferred_element_type=jnp.float32)
+            hidden[0:count, cols] = (g / (1.0 + jnp.exp(-g)) * u).astype(jnp.bfloat16)
+
+    def column(slot, side):
+        table = mix[slot, side]
+        row = lax.broadcasted_iota(jnp.int32, table.shape, 0)
+        line = jnp.sum(jnp.where(row == me, table, 0.0), axis=0, keepdims=True)
+        shape = (rows, table.shape[1])
+        same = lax.broadcasted_iota(jnp.int32, shape, 0) == lax.broadcasted_iota(jnp.int32, shape, 1)
+        return jnp.sum(jnp.where(same, line, 0.0), axis=1, keepdims=True)
+
+    def near_copy(slot):
+        dst = other_slot(slot)
+        return remote(away.at[slot], near.at[dst], near_send.at[dst], near_recv.at[dst], sibling)
+
+    def second_half(group):
+        count = len(group) * 2 * rows
+        scale = jnp.concatenate([column(slot, side) for slot in group for side in (0, 1)], axis=0)
+
+        @pl.loop(0, width // D_TILE)
+        def _(j):
+            cols = pl.ds(pl.multiple_of(j * D_TILE, D_TILE), D_TILE)
+            y = jnp.dot(hidden[0:count, :], vd[:, cols], preferred_element_type=jnp.float32)
+            y = y.astype(jnp.bfloat16).astype(jnp.float32) * scale
+            for i, slot in enumerate(group):
+                own[slot, :, cols] = y[2 * i * rows:(2 * i + 1) * rows]
+                away[slot, :, cols] = y[(2 * i + 1) * rows:(2 * i + 2) * rows].astype(jnp.bfloat16)
+
+        for slot in group:
+            start(near_copy(slot))
+
+    def await_near(slot):
+        remote(away.at[other_slot(slot)], near.at[slot], near_send.at[slot], near_recv.at[slot], sibling).wait_recv()
+
+    groups = [[0]] + [[long_slot(s), short_slot(s)] for s in range(1, RING // 2)] + [[RING - 1]]
+
+    for s in range(1, RING // 2 + 1):
+        arrive(s, (2, 0))
+        if s == 1:
+            for load in loads:
+                load.wait()
+        first_half(groups[s - 1])
+        arrive(s, (1,))
+        second_half(groups[s - 1])
+
+    def pass_on(k, far, slot_at, out_ref, in_ref, send, recv, e):
+        slot = slot_at(far - k)
+        if k == 0:
+            await_near(slot)
+        elif far - k:
+            await_near(slot)
+        for h in range(2):
+            at = pl.ds(h * half, half)
+            if k:
+                remote(out_ref.at[k - 1, at, :], in_ref.at[k - 1, at, :], send.at[k - 1, h], recv.at[k - 1, h], e).wait_recv()
+            total = own[slot, at, :] + near[slot, at, :].astype(jnp.float32)
+            if k:
+                total = total + in_ref[k - 1, at, :].astype(jnp.float32)
+            out_ref[k, at, :] = total.astype(jnp.bfloat16)
+            start(remote(out_ref.at[k, at, :], in_ref.at[k, at, :], send.at[k, h], recv.at[k, h], e))
+
+    def pass_long(k):
+        pass_on(k, RING // 2, long_slot, long_out, long_in, long_send, long_recv, behind)
+
+    def pass_short(k):
+        pass_on(k, RING // 2 - 1, short_slot, short_out, short_in, short_send, short_recv, ahead)
+
+    pass_short(0)
+    first_half(groups[-1])
+    second_half(groups[-1])
+    pass_long(0)
+    for k in range(1, RING // 2 - 1):
+        pass_short(k)
+        pass_long(k)
+    pass_long(RING // 2 - 1)
+
+    await_near(0)
+    last = RING // 2 - 1
+    for h in range(2):
+        at = pl.ds(h * half, half)
+        remote(short_out.at[last - 1, at, :], short_in.at[last - 1, at, :], short_send.at[last - 1, h], short_recv.at[last - 1, h], ahead).wait_recv()
+        remote(long_out.at[last, at, :], long_in.at[last, at, :], long_send.at[last, h], long_recv.at[last, h], behind).wait_recv()
+        total = own[0, at, :] + near[0, at, :].astype(jnp.float32)
+        total = total + short_in[last - 1, at, :].astype(jnp.float32) + long_in[last, at, :].astype(jnp.float32)
+        out[at, :] = total.astype(jnp.bfloat16)
+    for copy in sends:
+        copy.wait_send()
+
+
+def ring_local(tokens, router_probs, expert_ids, slot_expert, w_gate, w_up, w_down):
+    rows, width = tokens.shape
+    ff = w_gate.shape[2]
+    experts = slot_expert.shape[0]
+    hops = RING // 2
+    bf16, f32 = jnp.bfloat16, jnp.float32
+    dma = pltpu.SemaphoreType.DMA
+    vmem = pl.BlockSpec(memory_space=pltpu.VMEM)
+    hbm = pl.BlockSpec(memory_space=pl.ANY)
+    return pl.pallas_call(
+        kernel,
+        out_shape=jax.ShapeDtypeStruct((rows, width), bf16),
+        in_specs=[vmem, vmem, vmem, pl.BlockSpec(memory_space=pltpu.SMEM), hbm, hbm, hbm],
+        out_specs=vmem,
+        scratch_shapes=[
+            pltpu.VMEM((RING * 2 * rows, width), bf16),
+            pltpu.VMEM((RING, 2, experts, 128), f32),
+            pltpu.VMEM((width, ff), bf16),
+            pltpu.VMEM((width, ff), bf16),
+            pltpu.VMEM((ff, width), bf16),
+            pltpu.VMEM((4 * rows, ff), bf16),
+            pltpu.VMEM((RING, rows, width), f32),
+            pltpu.VMEM((RING, rows, width), bf16),
+            pltpu.VMEM((RING, rows, width), bf16),
+            pltpu.VMEM((hops, rows, width), bf16),
+            pltpu.VMEM((hops, rows, width), bf16),
+            pltpu.VMEM((hops - 1, rows, width), bf16),
+            pltpu.VMEM((hops - 1, rows, width), bf16),
+            dma((3,)),
+            dma((RING, 3)), dma((RING, 3)), dma((RING, 3)), dma((RING, 3)),
+            dma((RING,)), dma((RING,)),
+            dma((hops, 2)), dma((hops, 2)), dma((hops - 1, 2)), dma((hops - 1, 2)),
+        ],
+        compiler_params=pltpu.CompilerParams(
+            collective_id=0, has_side_effects=True, vmem_limit_bytes=50 * 2**20
+        ),
+        cost_estimate=pl.CostEstimate(
+            flops=6 * RING * 2 * rows * width * ff, bytes_accessed=6 * width * ff, transcendentals=0
+        ),
+    )(tokens, router_probs.T, expert_ids.T, slot_expert, w_gate, w_up, w_down)
+
+
 def solution(mesh):
     placed = (
         P(("groups", "expert", "sub"), None),
@@ -61,8 +327,9 @@
         P("expert", None, "sub"),
         P("expert", "sub", None),
     )
+    ring = mesh.shape["sub"] == 1 and mesh.shape["expert"] == 2 * RING
     return jax.shard_map(
-        local,
+        ring_local if ring else local,
         mesh=mesh,
         in_specs=placed,
         out_specs=P(("groups", "expert", "sub"), None),

time: 130 us -> 64.7 us (0.50)
  the two profiles are of different devices: /device:TPU:11 before, /device:TPU:0 now
where the time goes in v1:
time: 64.7 us; the launch traced here: 64.4 us
  Pallas kernels  58.8 us (91%)
  local copies, waits for them, and re-layouts  5.57 us (9%)
    pallas_call x1, Pallas kernels, ring_local(): pl.pallas_call(kernel, out_shape=jax.ShapeDtypeStruct((rows, width), bf16...  58.8 us
    unnamed x11, local copies, waits for them, and re-layouts  5.57 us

profile of v1, /device:TPU:0, one launch (start us, length us, event | category | flops | bytes accessed | tf_op | source)
XLA Modules:
  0.0 64.4 jit_solution(4178229780571818332)
XLA Ops:
  0.0 0.0 copy-start
  0.0 1.9 %copy-done = bf16[1,2048,768]{2,1,0:T(8,128)(2,1)S(1)} copy-done((bf16[1,2048,768]{2,1,0:T(8,128)(2,1)S(1)}, bf16[1,2048,768]{2,1,0:T(8,128)(2,1)}, u32[]{:S(2)}) %copy-start) | copy-done | bytes 3145752
  1.9 0.0 copy-start.1
  1.9 0.9 %copy-done.1 = bf16[64,2048]{1,0:T(8,128)(2,1)S(1)} copy-done((bf16[64,2048]{1,0:T(8,128)(2,1)S(1)}, bf16[64,2048]{1,0:T(8,128)(2,1)}, u32[]{:S(2)}) %copy-start.1) | copy-done | bytes 262168
  2.8 0.0 copy-start.2
  2.8 0.7 %copy-done.2 = f32[64,8]{0,1:T(8,128)S(1)} copy-done((f32[64,8]{0,1:T(8,128)S(1)}, f32[64,8]{0,1:T(8,128)}, u32[]{:S(2)}) %copy-start.2) | copy-done | bytes 2072
  3.5 0.0 copy-start.3
  3.5 0.7 %copy-done.3 = s32[64,8]{0,1:T(8,128)S(1)} copy-done((s32[64,8]{0,1:T(8,128)S(1)}, s32[64,8]{0,1:T(8,128)}, u32[]{:S(2)}) %copy-start.3) | copy-done | bytes 2072
  4.2 0.0 copy-start.4
  4.2 0.7 %copy-done.4 = s32[16]{0:T(128)S(1)} copy-done((s32[16]{0:T(128)S(1)}, s32[16]{0:T(128)}, u32[]{:S(2)}) %copy-start.4) | copy-done | bytes 88
  4.9 58.8 %shard_map.73 = bf16[64,2048]{1,0:T(8,128)(2,1)S(1)} custom-call(bf16[64,2048]{1,0:T(8,128)(2,1)S(1)} %copy-done.1, f32[8,64]{1,0:T(8,128)S(1)} %bitcast.2, s32[8,64]{1,0:T(8,128)S(1)} %bitcast.3, s32[16]{0:T(128)S(1)} %copy-done.4, bf16[1,2048,768]{2,1,0:T(8,128)(2,1)S(1)} %copy-done, bf16[1,2048,768]{2,1,0:T(8,128)(2,1)} %w_up.1, bf16[1,768,2048]{2,1,0:T(8,128)(2,1)} %w_down.1), custom_call_target="tpu_custom_call" | custom-call | flops 9663676416 | bytes 9437184 | tf_op jit(solution)/shard_map/pallas_call | solution.py:287
  63.7 0.7 %copy.9 = bf16[64,2048]{1,0:T(8,128)(2,1)} copy(bf16[64,2048]{1,0:T(8,128)(2,1)S(1)} %shard_map.73) | data formatting | bytes 524288
Async XLA Ops:
  0.0 1.9 %copy-start = (bf16[1,2048,768]{2,1,0:T(8,128)(2,1)S(1)}, bf16[1,2048,768]{2,1,0:T(8,128)(2,1)}, u32[]{:S(2)}) copy-start(bf16[1,2048,768]{2,1,0:T(8,128)(2,1)} %w_gate.1) | copy-start | bytes 9437188
  1.9 0.9 %copy-start.1 = (bf16[64,2048]{1,0:T(8,128)(2,1)S(1)}, bf16[64,2048]{1,0:T(8,128)(2,1)}, u32[]{:S(2)}) copy-start(bf16[64,2048]{1,0:T(8,128)(2,1)} %tokens.1) | copy-start | bytes 786436
  2.8 0.7 %copy-start.2 = (f32[64,8]{0,1:T(8,128)S(1)}, f32[64,8]{0,1:T(8,128)}, u32[]{:S(2)}) copy-start(f32[64,8]{0,1:T(8,128)} %param.8) | copy-start | bytes 6148
  3.5 0.7 %copy-start.3 = (s32[64,8]{0,1:T(8,128)S(1)}, s32[64,8]{0,1:T(8,128)}, u32[]{:S(2)}) copy-start(s32[64,8]{0,1:T(8,128)} %param.9) | copy-start | bytes 6148
  4.2 0.7 %copy-start.4 = (s32[16]{0:T(128)S(1)}, s32[16]{0:T(128)}, u32[]{:S(2)}) copy-start(s32[16]{0:T(128)} %slots.1) | copy-start | bytes 196

commit v2 on v1

--- a/solution.py
+++ b/solution.py
@@ -1,3 +1,5 @@
+import functools
+
 import jax
 import jax.numpy as jnp
 from jax import lax
@@ -6,6 +8,7 @@
 from jax.sharding import PartitionSpec as P
 
 RING = 8
+PARTS = 2
 FF_TILE = 256
 D_TILE = 512
 
@@ -83,13 +86,13 @@
 
 
 def kernel(
-    tokens, probs, ids, slots, w_gate, w_up, w_down, out,
-    x, mix, vg, vu, vd, hidden, own, away, near, long_out, long_in, short_out, short_in,
-    w_sem, ag_send, ag_recv, sib_send, sib_recv, near_send, near_recv,
+    tokens, probs_in, ids_in, slots_in, w_gate, w_up, w_down, out,
+    probs, ids, slots, x, mix, vg, vu, vd, hidden, own, away, near, long_out, long_in, short_out, short_in,
+    in_sem, w_sem, ag_send, ag_recv, sib_send, sib_recv, near_send, near_recv,
     long_send, long_recv, short_send, short_recv,
 ):
     rows, width = tokens.shape
-    half = rows // 2
+    half = rows // PARTS
     ff = hidden.shape[1]
     me = lax.axis_index("expert")
     place, core = ring_place(me)
@@ -111,15 +114,55 @@
     for e in (ahead, behind, sibling):
         pl.semaphore_signal(barrier, inc=1, device_id=device(e), device_id_type=pl.DeviceIdType.MESH)
 
+    smalls = [
+        pltpu.make_async_copy(probs_in, probs, in_sem.at[0]),
+        pltpu.make_async_copy(ids_in, ids, in_sem.at[1]),
+        pltpu.make_async_copy(slots_in, slots, in_sem.at[2]),
+    ]
     loads = [
-        pltpu.make_async_copy(w_gate.at[0], vg, w_sem.at[0]),
-        pltpu.make_async_copy(w_up.at[0], vu, w_sem.at[1]),
-        pltpu.make_async_copy(w_down.at[0], vd, w_sem.at[2]),
+        pltpu.make_async_copy(tokens, x.at[pl.ds(0, rows), :], w_sem.at[0]),
+        pltpu.make_async_copy(w_gate.at[0], vg, w_sem.at[1]),
+        pltpu.make_async_copy(w_up.at[0], vu, w_sem.at[2]),
+        pltpu.make_async_copy(w_down.at[0], vd, w_sem.at[3]),
     ]
+    for load in smalls:
+        load.start()
+
+    pl.semaphore_wait(barrier, 3)
+
+    def view(slot, side, part):
+        if part == PARTS:
+            return mix.at[slot, side]
+        return x.at[pl.ds(slot * 2 * rows + side * rows + part * half, half), :]
+
+    def held_at(slot, part):
+        if slot == 0 and part < PARTS:
+            return tokens.at[pl.ds(part * half, half), :]
+        return view(slot, 0, part)
+
+    sends = []
+
+    def ring_copy(src, dst, part, e):
+        return remote(held_at(src, part), view(dst, 0, part), ag_send.at[dst, part], ag_recv.at[dst, part], e)
+
+    def sib_copy(slot, part):
+        dst = other_slot(slot)
+        return remote(held_at(slot, part), view(dst, 1, part), sib_send.at[dst, part], sib_recv.at[dst, part], sibling)
+
+    def start(copy):
+        copy.start()
+        sends.append(copy)
+
+    for part in range(PARTS):
+        start(ring_copy(0, long_slot(1), part, ahead))
+        start(ring_copy(0, short_slot(1), part, behind))
+    for part in range(PARTS):
+        start(sib_copy(0, part))
     for load in loads:
         load.start()
-
-    x[0:rows, :] = tokens[...]
+    for load in smalls:
+        load.wait()
+
     p = probs[...]
     gates = p / jnp.sum(p, axis=0, keepdims=True)
     experts = mix.shape[2]
@@ -132,36 +175,12 @@
         weight = weight + jnp.where(ids[k:k + 1, :] == held, gates[k:k + 1, :], 0.0)
     mix[0, 0, :, 0:rows] = weight
     mix[0, 0, :, rows:] = jnp.zeros((experts, mix.shape[3] - rows), jnp.float32)
-
-    pl.semaphore_wait(barrier, 3)
-
-    def view(slot, side, part):
-        if part == 2:
-            return mix.at[slot, side]
-        return x.at[pl.ds(slot * 2 * rows + side * rows + part * half, half), :]
-
-    PARTS = (2, 0, 1)
-    sends = []
-
-    def ring_copy(src, dst, part, e):
-        return remote(view(src, 0, part), view(dst, 0, part), ag_send.at[dst, part], ag_recv.at[dst, part], e)
-
-    def sib_copy(slot, part):
-        dst = other_slot(slot)
-        return remote(view(slot, 0, part), view(dst, 1, part), sib_send.at[dst, part], sib_recv.at[dst, part], sibling)
-
-    def start(copy):
-        copy.start()
-        sends.append(copy)
-
-    for part in PARTS:
-        start(ring_copy(0, long_slot(1), part, ahead))
-        start(ring_copy(0, short_slot(1), part, behind))
-    for part in PARTS:
-        start(sib_copy(0, part))
+    start(ring_copy(0, long_slot(1), PARTS, ahead))
+    start(ring_copy(0, short_slot(1), PARTS, behind))
+    start(sib_copy(0, PARTS))
 
     def await_sib(slot, part):
-        remote(view(other_slot(slot), 0, part), view(slot, 1, part), sib_send.at[slot, part], sib_recv.at[slot, part], sibling).wait_recv()
+        remote(held_at(other_slot(slot), part), view(slot, 1, part), sib_send.at[slot, part], sib_recv.at[slot, part], sibling).wait_recv()
 
     def arrive(s, parts):
         for part in parts:
@@ -175,19 +194,24 @@
                     start(ring_copy(short_slot(s), short_slot(s + 1), part, behind))
                 start(sib_copy(short_slot(s), part))
 
-    def first_half(group):
-        for slot in group:
-            for part in PARTS:
-                await_sib(slot, part)
+    def first_items(group):
         base, count = group[0] * 2 * rows, len(group) * 2 * rows
 
-        @pl.loop(0, ff // FF_TILE)
-        def _(j):
-            cols = pl.ds(pl.multiple_of(j * FF_TILE, FF_TILE), FF_TILE)
+        def ready():
+            for slot in group:
+                for part in range(PARTS):
+                    await_sib(slot, part)
+
+        def tile(j):
+            if j == 0:
+                ready()
+            cols = pl.ds(j * FF_TILE, FF_TILE)
             a = x[base:base + count, :]
             g = jnp.dot(a, vg[:, cols], preferred_element_type=jnp.float32)
             u = jnp.dot(a, vu[:, cols], preferred_element_type=jnp.float32)
             hidden[0:count, cols] = (g / (1.0 + jnp.exp(-g)) * u).astype(jnp.bfloat16)
+
+        return [functools.partial(tile, j) for j in range(ff // FF_TILE)]
 
     def column(slot, side):
         table = mix[slot, side]
@@ -201,21 +225,26 @@
         dst = other_slot(slot)
         return remote(away.at[slot], near.at[dst], near_send.at[dst], near_recv.at[dst], sibling)
 
-    def second_half(group):
+    def second_items(group):
         count = len(group) * 2 * rows
-        scale = jnp.concatenate([column(slot, side) for slot in group for side in (0, 1)], axis=0)
-
-        @pl.loop(0, width // D_TILE)
-        def _(j):
-            cols = pl.ds(pl.multiple_of(j * D_TILE, D_TILE), D_TILE)
+        scale = []
+
+        def tile(j):
+            if j == 0:
+                for slot in group:
+                    await_sib(slot, PARTS)
+                scale.append(jnp.concatenate([column(slot, side) for slot in group for side in (0, 1)], axis=0))
+            cols = pl.ds(j * D_TILE, D_TILE)
             y = jnp.dot(hidden[0:count, :], vd[:, cols], preferred_element_type=jnp.float32)
-            y = y.astype(jnp.bfloat16).astype(jnp.float32) * scale
+            y = y.astype(jnp.bfloat16).astype(jnp.float32) * scale[0]
             for i, slot in enumerate(group):
                 own[slot, :, cols] = y[2 * i * rows:(2 * i + 1) * rows]
                 away[slot, :, cols] = y[(2 * i + 1) * rows:(2 * i + 2) * rows].astype(jnp.bfloat16)
-
-        for slot in group:
-            start(near_copy(slot))
+            if j == width // D_TILE - 1:
+                for slot in group:
+                    start(near_copy(slot))
+
+        return [functools.partial(tile, j) for j in range(width // D_TILE)]
 
     def await_near(slot):
         remote(away.at[other_slot(slot)], near.at[slot], near_send.at[slot], near_recv.at[slot], sibling).wait_recv()
@@ -223,13 +252,14 @@
     groups = [[0]] + [[long_slot(s), short_slot(s)] for s in range(1, RING // 2)] + [[RING - 1]]
 
     for s in range(1, RING // 2 + 1):
-        arrive(s, (2, 0))
-        if s == 1:
-            for load in loads:
-                load.wait()
-        first_half(groups[s - 1])
-        arrive(s, (1,))
-        second_half(groups[s - 1])
+        items = first_items(groups[s - 1]) + second_items(groups[s - 1])
+        for part in range(PARTS):
+            arrive(s, (part,) if part else (part, PARTS))
+            if s == 1 and part == 0:
+                for load in loads:
+                    load.wait()
+            for item in items[len(items) * part // PARTS:len(items) * (part + 1) // PARTS]:
+                item()
 
     def pass_on(k, far, slot_at, out_ref, in_ref, send, recv, e):
         slot = slot_at(far - k)
@@ -237,7 +267,7 @@
             await_near(slot)
         elif far - k:
             await_near(slot)
-        for h in range(2):
+        for h in range(PARTS):
             at = pl.ds(h * half, half)
             if k:
                 remote(out_ref.at[k - 1, at, :], in_ref.at[k - 1, at, :], send.at[k - 1, h], recv.at[k - 1, h], e).wait_recv()
@@ -254,8 +284,8 @@
         pass_on(k, RING // 2 - 1, short_slot, short_out, short_in, short_send, short_recv, ahead)
 
     pass_short(0)
-    first_half(groups[-1])
-    second_half(groups[-1])
+    for item in first_items(groups[-1]) + second_items(groups[-1]):
+        item()
     pass_long(0)
     for k in range(1, RING // 2 - 1):
         pass_short(k)
@@ -264,7 +294,7 @@
 
     await_near(0)
     last = RING // 2 - 1
-    for h in range(2):
+    for h in range(PARTS):
         at = pl.ds(h * half, half)
         remote(short_out.at[last - 1, at, :], short_in.at[last - 1, at, :], short_send.at[last - 1, h], short_recv.at[last - 1, h], ahead).wait_recv()
         remote(long_out.at[last, at, :], long_in.at[last, at, :], long_send.at[last, h], long_recv.at[last, h], behind).wait_recv()
@@ -287,9 +317,12 @@
     return pl.pallas_call(
         kernel,
         out_shape=jax.ShapeDtypeStruct((rows, width), bf16),
-        in_specs=[vmem, vmem, vmem, pl.BlockSpec(memory_space=pltpu.SMEM), hbm, hbm, hbm],
+        in_specs=[hbm] * 7,
         out_specs=vmem,
         scratch_shapes=[
+            pltpu.VMEM(router_probs.shape[::-1], f32),
+            pltpu.VMEM(expert_ids.shape[::-1], jnp.int32),
+            pltpu.SMEM(slot_expert.shape, jnp.int32),
             pltpu.VMEM((RING * 2 * rows, width), bf16),
             pltpu.VMEM((RING, 2, experts, 128), f32),
             pltpu.VMEM((width, ff), bf16),
@@ -303,13 +336,13 @@
             pltpu.VMEM((hops, rows, width), bf16),
             pltpu.VMEM((hops - 1, rows, width), bf16),
             pltpu.VMEM((hops - 1, rows, width), bf16),
-            dma((3,)),
-            dma((RING, 3)), dma((RING, 3)), dma((RING, 3)), dma((RING, 3)),
+            dma((3,)), dma((4,)),
+            dma((RING, PARTS + 1)), dma((RING, PARTS + 1)), dma((RING, PARTS + 1)), dma((RING, PARTS + 1)),
             dma((RING,)), dma((RING,)),
-            dma((hops, 2)), dma((hops, 2)), dma((hops - 1, 2)), dma((hops - 1, 2)),
+            dma((hops, PARTS)), dma((hops, PARTS)), dma((hops - 1, PARTS)), dma((hops - 1, PARTS)),
         ],
         compiler_params=pltpu.CompilerParams(
-            collective_id=0, has_side_effects=True, vmem_limit_bytes=50 * 2**20
+            collective_id=0, has_side_effects=True, vmem_limit_bytes=60 * 2**20
         ),
         cost_estimate=pl.CostEstimate(
             flops=6 * RING * 2 * rows * width * ff, bytes_accessed=6 * width * ff, transcendentals=0

time: 64.7 us -> 58.4 us (0.903)
  local copies, waits for them, and re-layouts: 5.57 us -> 1.67 us
  Pallas kernels: 58.8 us -> 56.5 us
    unnamed x11 -> x1, local copies, waits for them, and re-layouts: 5.57 us -> 1.67 us
    pallas_call x1, Pallas kernels: 58.8 us -> 56.5 us  [ring_local(): pl.pallas_call(kernel, out_shape=jax.ShapeDtypeStruct((rows, width), bf16...]
where the time goes in v2:
time: 58.4 us; the launch traced here: 58.2 us
  Pallas kernels  56.5 us (97%)
  local copies, waits for them, and re-layouts  1.67 us (3%)
    pallas_call x1, Pallas kernels, ring_local(): pl.pallas_call(kernel, out_shape=jax.ShapeDtypeStruct((rows, width), bf16...  56.5 us
    unnamed x1, local copies, waits for them, and re-layouts  1.67 us

profile of v2, /device:TPU:0, one launch (start us, length us, event | category | flops | bytes accessed | tf_op | source)
XLA Modules:
  0.0 58.2 jit_solution(944771002692839497)
XLA Ops:
  0.0 56.5 %shard_map.73 = bf16[64,2048]{1,0:T(8,128)(2,1)} custom-call(bf16[64,2048]{1,0:T(8,128)(2,1)} %tokens.1, f32[8,64]{1,0:T(8,128)} %bitcast.2, s32[8,64]{1,0:T(8,128)} %bitcast.3, s32[16]{0:T(128)} %slots_in.1, bf16[1,2048,768]{2,1,0:T(8,128)(2,1)} %w_gate.1, bf16[1,2048,768]{2,1,0:T(8,128)(2,1)} %w_up.1, bf16[1,768,2048]{2,1,0:T(8,128)(2,1)} %w_down.1), custom_call_target="tpu_custom_call" | custom-call | flops 9663676416 | bytes 9437184 | tf_op jit(solution)/shard_map/pallas_call | solution.py:317
  56.6 1.7 %copy.9 = bf16[64,2048]{1,0:T(8,128)(2,1)} copy(bf16[64,2048]{1,0:T(8,128)(2,1)} %shard_map.73) | data formatting | bytes 524288

commit v3 on v2

--- a/solution.py
+++ b/solution.py
@@ -86,10 +86,11 @@
 
 
 def kernel(
-    tokens, probs_in, ids_in, slots_in, w_gate, w_up, w_down, out,
+    tokens, probs_in, ids_in, slots_in, w_gate, w_up, w_down, out, last_in,
     probs, ids, slots, x, mix, vg, vu, vd, hidden, own, away, near, long_out, long_in, short_out, short_in,
     in_sem, w_sem, ag_send, ag_recv, sib_send, sib_recv, near_send, near_recv,
     long_send, long_recv, short_send, short_recv,
+    rest, out_sem,
 ):
     rows, width = tokens.shape
     half = rows // PARTS
@@ -140,7 +141,7 @@
             return tokens.at[pl.ds(part * half, half), :]
         return view(slot, 0, part)
 
-    sends = []
+    sends, stores = [], []
 
     def ring_copy(src, dst, part, e):
         return remote(held_at(src, part), view(dst, 0, part), ag_send.at[dst, part], ag_recv.at[dst, part], e)
@@ -275,7 +276,8 @@
             if k:
                 total = total + in_ref[k - 1, at, :].astype(jnp.float32)
             out_ref[k, at, :] = total.astype(jnp.bfloat16)
-            start(remote(out_ref.at[k, at, :], in_ref.at[k, at, :], send.at[k, h], recv.at[k, h], e))
+            landing = last_in.at[at, :] if k == RING // 2 - 1 else in_ref.at[k, at, :]
+            start(remote(out_ref.at[k, at, :], landing, send.at[k, h], recv.at[k, h], e))
 
     def pass_long(k):
         pass_on(k, RING // 2, long_slot, long_out, long_in, long_send, long_recv, behind)
@@ -283,8 +285,10 @@
     def pass_short(k):
         pass_on(k, RING // 2 - 1, short_slot, short_out, short_in, short_send, short_recv, ahead)
 
+    for item in first_items(groups[-1]):
+        item()
     pass_short(0)
-    for item in first_items(groups[-1]) + second_items(groups[-1]):
+    for item in second_items(groups[-1]):
         item()
     pass_long(0)
     for k in range(1, RING // 2 - 1):
@@ -297,10 +301,16 @@
     for h in range(PARTS):
         at = pl.ds(h * half, half)
         remote(short_out.at[last - 1, at, :], short_in.at[last - 1, at, :], short_send.at[last - 1, h], short_recv.at[last - 1, h], ahead).wait_recv()
-        remote(long_out.at[last, at, :], long_in.at[last, at, :], long_send.at[last, h], long_recv.at[last, h], behind).wait_recv()
         total = own[0, at, :] + near[0, at, :].astype(jnp.float32)
-        total = total + short_in[last - 1, at, :].astype(jnp.float32) + long_in[last, at, :].astype(jnp.float32)
-        out[at, :] = total.astype(jnp.bfloat16)
+        rest[at, :] = total + short_in[last - 1, at, :].astype(jnp.float32)
+        store = pltpu.make_async_copy(rest.at[at, :], out.at[at, :], out_sem.at[h])
+        store.start()
+        stores.append(store)
+    for h in range(PARTS):
+        at = pl.ds(h * half, half)
+        remote(long_out.at[last, at, :], last_in.at[at, :], long_send.at[last, h], long_recv.at[last, h], behind).wait_recv()
+    for store in stores:
+        store.wait()
     for copy in sends:
         copy.wait_send()
 
@@ -312,13 +322,12 @@
     hops = RING // 2
     bf16, f32 = jnp.bfloat16, jnp.float32
     dma = pltpu.SemaphoreType.DMA
-    vmem = pl.BlockSpec(memory_space=pltpu.VMEM)
     hbm = pl.BlockSpec(memory_space=pl.ANY)
-    return pl.pallas_call(
+    here, arrived = pl.pallas_call(
         kernel,
-        out_shape=jax.ShapeDtypeStruct((rows, width), bf16),
+        out_shape=(jax.ShapeDtypeStruct((rows, width), f32), jax.ShapeDtypeStruct((rows, width), bf16)),
         in_specs=[hbm] * 7,
-        out_specs=vmem,
+        out_specs=(hbm, hbm),
         scratch_shapes=[
             pltpu.VMEM(router_probs.shape[::-1], f32),
             pltpu.VMEM(expert_ids.shape[::-1], jnp.int32),
@@ -333,13 +342,14 @@
             pltpu.VMEM((RING, rows, width), bf16),
             pltpu.VMEM((RING, rows, width), bf16),
             pltpu.VMEM((hops, rows, width), bf16),
-            pltpu.VMEM((hops, rows, width), bf16),
+            pltpu.VMEM((hops - 1, rows, width), bf16),
             pltpu.VMEM((hops - 1, rows, width), bf16),
             pltpu.VMEM((hops - 1, rows, width), bf16),
             dma((3,)), dma((4,)),
             dma((RING, PARTS + 1)), dma((RING, PARTS + 1)), dma((RING, PARTS + 1)), dma((RING, PARTS + 1)),
             dma((RING,)), dma((RING,)),
             dma((hops, PARTS)), dma((hops, PARTS)), dma((hops - 1, PARTS)), dma((hops - 1, PARTS)),
+            pltpu.VMEM((rows, width), f32), dma((PARTS,)),
         ],
         compiler_params=pltpu.CompilerParams(
             collective_id=0, has_side_effects=True, vmem_limit_bytes=60 * 2**20
@@ -348,6 +358,7 @@
             flops=6 * RING * 2 * rows * width * ff, bytes_accessed=6 * width * ff, transcendentals=0
         ),
     )(tokens, router_probs.T, expert_ids.T, slot_expert, w_gate, w_up, w_down)
+    return (here + arrived.astype(f32)).astype(bf16)
 
 
 def solution(mesh):

time: 58.4 us -> 56.8 us (0.973)
  other arithmetic: 0 us -> 1.86 us
  Pallas kernels: 56.5 us -> 54.8 us
  local copies, waits for them, and re-layouts: 1.67 us -> 0 us
    convert_element_type x0 -> x1, other arithmetic: none -> 1.86 us  [ring_local(): return (here + arrived.astype(f32)).astype(bf16)]
    pallas_call x1, Pallas kernels: 56.5 us -> 54.8 us  [ring_local(): pl.pallas_call(kernel, out_shape=(jax.ShapeDtypeStruct((rows, width), f32...]
    unnamed x1 -> x0, local copies, waits for them, and re-layouts: 1.67 us -> none
where the time goes in v3:
time: 56.8 us; the launch traced here: 56.6 us
  Pallas kernels  54.8 us (96%)
  other arithmetic  1.86 us (3%)
    pallas_call x1, Pallas kernels, ring_local(): pl.pallas_call(kernel, out_shape=(jax.ShapeDtypeStruct((rows, width), f32...  54.8 us
    convert_element_type x1, other arithmetic, ring_local(): return (here + arrived.astype(f32)).astype(bf16)  1.86 us

profile of v3, /device:TPU:0, one launch (start us, length us, event | category | flops | bytes accessed | tf_op | source)
XLA Modules:
  0.0 56.6 jit_solution(5203056929482024224)
XLA Ops:
  0.0 54.8 %shard_map.73 = (f32[64,2048]{1,0:T(8,128)}, bf16[64,2048]{1,0:T(8,128)(2,1)}) custom-call(bf16[64,2048]{1,0:T(8,128)(2,1)} %tokens.1, f32[8,64]{1,0:T(8,128)} %bitcast.2, s32[8,64]{1,0:T(8,128)} %bitcast.3, s32[16]{0:T(128)} %slots_in.1, bf16[1,2048,768]{2,1,0:T(8,128)(2,1)} %w_gate.1, bf16[1,2048,768]{2,1,0:T(8,128)(2,1)} %w_up.1, bf16[1,768,2048]{2,1,0:T(8,128)(2,1)} %w_down.1), custom_call_target="tpu_custom_call" | custom-call | flops 9663676416 | bytes 9437184 | tf_op jit(solution)/shard_map/pallas_call | solution.py:326
  54.8 1.9 %add_convert_fusion = bf16[64,2048]{1,0:T(8,128)(2,1)} fusion(f32[64,2048]{1,0:T(8,128)} %get-tuple-element.7, bf16[64,2048]{1,0:T(8,128)(2,1)} %get-tuple-element.8), kind=kLoop, calls=%fused_computation | loop fusion | flops 393216 | bytes 1048576 | tf_op jit(solution)/shard_map/convert_element_type | solution.py:361

commit v4 on v3

--- a/solution.py
+++ b/solution.py
@@ -188,11 +188,13 @@
             ring_copy(long_slot(s - 1), long_slot(s), part, ahead).wait_recv()
             if s < RING // 2:
                 start(ring_copy(long_slot(s), long_slot(s + 1), part, ahead))
-            start(sib_copy(long_slot(s), part))
+            else:
+                start(sib_copy(long_slot(s), part))
             if s < RING // 2:
                 ring_copy(short_slot(s - 1), short_slot(s), part, behind).wait_recv()
                 if s < RING // 2 - 1:
                     start(ring_copy(short_slot(s), short_slot(s + 1), part, behind))
+                start(sib_copy(long_slot(s), part))
                 start(sib_copy(short_slot(s), part))
 
     def first_items(group):

time: 56.8 us -> 56.7 us (level)
  no operation moved by 1% of the time
where the time goes in v4:
time: 56.7 us; the launch traced here: 56.6 us
  Pallas kernels  54.7 us (96%)
  other arithmetic  1.86 us (3%)
    pallas_call x1, Pallas kernels, ring_local(): pl.pallas_call(kernel, out_shape=(jax.ShapeDtypeStruct((rows, width), f32...  54.7 us
    convert_element_type x1, other arithmetic, ring_local(): return (here + arrived.astype(f32)).astype(bf16)  1.86 us

profile of v4, /device:TPU:0, one launch (start us, length us, event | category | flops | bytes accessed | tf_op | source)
XLA Modules:
  0.0 56.6 jit_solution(11171762161786522132)
XLA Ops:
  0.0 54.7 %shard_map.73 = (f32[64,2048]{1,0:T(8,128)}, bf16[64,2048]{1,0:T(8,128)(2,1)}) custom-call(bf16[64,2048]{1,0:T(8,128)(2,1)} %tokens.1, f32[8,64]{1,0:T(8,128)} %bitcast.2, s32[8,64]{1,0:T(8,128)} %bitcast.3, s32[16]{0:T(128)} %slots_in.1, bf16[1,2048,768]{2,1,0:T(8,128)(2,1)} %w_gate.1, bf16[1,2048,768]{2,1,0:T(8,128)(2,1)} %w_up.1, bf16[1,768,2048]{2,1,0:T(8,128)(2,1)} %w_down.1), custom_call_target="tpu_custom_call" | custom-call | flops 9663676416 | bytes 9437184 | tf_op jit(solution)/shard_map/pallas_call | solution.py:328
  54.7 1.9 %add_convert_fusion = bf16[64,2048]{1,0:T(8,128)(2,1)} fusion(f32[64,2048]{1,0:T(8,128)} %get-tuple-element.7, bf16[64,2048]{1,0:T(8,128)(2,1)} %get-tuple-element.8), kind=kLoop, calls=%fused_computation | loop fusion | flops 393216 | bytes 1048576 | tf_op jit(solution)/shard_map/convert_element_type | solution.py:363
